TPU v7x, 128 devices: a whole 4x4x4 slice. The times are simulated.
128 devices in a mesh: dp: 32 (over z, x, core), grp: 4 (over y).
Axes of the slice: x: 4, y: 4, z: 4, core: 2. Of those that a mesh axis runs over, the one named last changes fastest.
Arguments:
- features: bfloat16 [16384, 1024], P(('dp', 'grp')), may hold values from -24 to 24
- proj_weight: bfloat16 [1024, 512], replicated, may hold values from -0.01171875 to 0.01171875
- labels: int32 [16384], P(('dp', 'grp')), may hold values from 0 to 511, as said below
- owner_slot: int32 [512], replicated, may hold values from 0 to 511, each once
Outputs:
- projected_grad: bfloat16 [16384, 512], P(('dp', 'grp'))
- weight_grad: float32 [1024, 512], P(('dp', 'grp'))
- owned_sums: float32 [512, 512], P(('dp', 'grp'))
Inputs may be any that keep to these rules, and one draw needn't show every extreme that they name: `labels`: every class of 0 to 511 has 1 to 64 rows, some class exactly 64; rows of a class lie anywhere in the batch. `owner_slot`: A permutation.
All inputs are finite; a program needn't handle non-finite values.
Results may differ from a plain program's by a relative error of at most 0.0036.
The roundings to bfloat16 on the way count: a program that leaves them out, or rounds other values in their place, can miss the bound.
Values may be sent and summed in bfloat16 or wider, within the bound.
A program may use at most 128 MiB of HBM per device.

v0:
```python
import jax
import jax.numpy as jnp
from jax import lax
from jax.sharding import PartitionSpec as P

sharpness_divisor = 0.1


def local_partials(labels, owner_slot, unit_vectors_brain16, class_range):
    label_hot = labels[:, None] == class_range[None, :]
    row_slot = jnp.sum(jnp.where(label_hot, owner_slot[None, :], 0), axis=1)
    slot_hot = row_slot[:, None] == class_range[None, :]
    partial_value = lax.dot_general(
        slot_hot.astype(jnp.bfloat16),
        unit_vectors_brain16,
        (((0,), (0,)), ((), ())),
        preferred_element_type=jnp.float32,
    )
    part_count = jnp.sum(slot_hot.astype(jnp.float32), axis=0)
    return (slot_hot.astype(jnp.float32), partial_value, part_count)


def body(features, proj_weight, labels, owner_slot):
    row_count = features.shape[0]
    devices = lax.axis_size(("dp", "grp"))
    total_rows = row_count * devices
    class_total = owner_slot.shape[0]
    projected = jnp.dot(features, proj_weight, preferred_element_type=jnp.float32)
    inv_norm = lax.rsqrt(jnp.sum(projected * projected, axis=1, keepdims=True) + 1e-06)
    unit = projected * inv_norm
    unit_vectors_brain16 = unit.astype(jnp.bfloat16)
    gathered = lax.all_gather(unit_vectors_brain16, ("dp", "grp"), axis=0, tiled=True)
    my_index = lax.axis_index(("dp", "grp"))
    first_row = my_index * row_count
    cosine_score_matrix = (
        lax.dot_general(
            unit_vectors_brain16,
            gathered,
            (((1,), (1,)), ((), ())),
            preferred_element_type=jnp.float32,
        )
        / sharpness_divisor
    )
    col_index = jnp.arange(total_rows, dtype=jnp.int32)
    self_mask = col_index[None, :] == (first_row + jnp.arange(row_count, dtype=jnp.int32))[:, None]
    exp_terms = jnp.where(self_mask, jnp.float32(0.0), jnp.exp(cosine_score_matrix))
    log_total = jnp.log(jnp.sum(exp_terms, axis=1))
    class_range = jnp.arange(class_total, dtype=jnp.int32)
    slot_wide, partial_value, part_count = local_partials(
        labels, owner_slot, unit_vectors_brain16, class_range
    )
    owned_sums, owned_count = (
        lax.psum_scatter(partial_value, ("dp", "grp"), scatter_dimension=0, tiled=True),
        lax.psum_scatter(part_count, ("dp", "grp"), scatter_dimension=0, tiled=True),
    )
    class_sums, class_count = (
        lax.all_gather(owned_sums, ("dp", "grp"), axis=0, tiled=True),
        lax.all_gather(owned_count, ("dp", "grp"), axis=0, tiled=True),
    )
    anchor_category_ids = jnp.dot(
        slot_wide, class_sums, precision=lax.Precision.HIGHEST, preferred_element_type=jnp.float32
    )
    row_total_count = jnp.dot(
        slot_wide, class_count, precision=lax.Precision.HIGHEST, preferred_element_type=jnp.float32
    )
    same_category_tally = jnp.maximum(row_total_count - 1.0, 1.0)
    unit_vectors_single_precise = unit_vectors_brain16.astype(jnp.float32)
    row_prob = jnp.where(
        self_mask, jnp.float32(0.0), jnp.exp(cosine_score_matrix - log_total[:, None])
    ).astype(jnp.bfloat16)
    anchor_side_share = jnp.dot(row_prob, gathered, preferred_element_type=jnp.float32)
    cols = row_prob
    target_side_share = lax.psum_scatter(
        lax.dot_general(
            cols, unit_vectors_brain16, (((0,), (0,)), ((), ())), preferred_element_type=jnp.float32
        ),
        ("dp", "grp"),
        scatter_dimension=0,
        tiled=True,
    )
    feature_vector_derivative = (
        anchor_side_share + target_side_share
    ) / sharpness_divisor - 2.0 * (anchor_category_ids - unit_vectors_single_precise) / (
        sharpness_divisor * same_category_tally[:, None]
    )
    radial = jnp.sum(unit * feature_vector_derivative, axis=1, keepdims=True)
    projected_grad = (inv_norm * (feature_vector_derivative - unit * radial)).astype(jnp.bfloat16)
    cols = features
    weight_grad = lax.psum_scatter(
        lax.dot_general(
            cols, projected_grad, (((0,), (0,)), ((), ())), preferred_element_type=jnp.float32
        ),
        ("dp", "grp"),
        scatter_dimension=0,
        tiled=True,
    )
    return (projected_grad, weight_grad, owned_sums)


def solution(mesh):
    in_specs = (P(("dp", "grp"), None), P(), P(("dp", "grp")), P())
    out_specs = (P(("dp", "grp"), None), P(("dp", "grp"), None), P(("dp", "grp"), None))
    return jax.shard_map(body, mesh=mesh, in_specs=in_specs, out_specs=out_specs, check_vma=False)
```

profile of v0, /device:TPU:0, one launch (start us, length us, event | category | flops | bytes accessed | tf_op | source)
XLA Modules:
  0.0 1665.8 jit_solution(7402861398737213482)
XLA Ops:
  7.2 1.2 copy-done
  8.4 1.3 multiply_reduce_fusion.1
  9.9 0.9 select_reduce_fusion.1
  10.8 1.4 fusion.7
  12.3 0.7 all-gather.4.cloned.1.call-update
  13.0 149.0 %all-reduce.5.cloned.1.call-done = f32[512,512]{1,0:T(8,128)} async-done(((f32[512,512]{1,0:T(8,128)}), f32[512,512]{1,0:T(8,128)}) %all-reduce.5.cloned.1.call-update) | async-done | bytes 1048592
  162.0 1.3 fusion.23
  163.4 82.4 %all-gather.4.cloned.1.call-done = bf16[16384,512]{1,0:T(8,128)(2,1)} async-done(((bf16[128,512]{1,0:T(8,128)(2,1)}), bf16[16384,512]{1,0:T(8,128)(2,1)}) %all-gather.4.cloned.1.call-update) | async-done | bytes 16777232 | tf_op jit(solution)/shard_map/all_gather | solution.py:32
  245.8 14.9 select_reduce_fusion
  260.7 17.2 %fusion.11 = f32[16384,512]{1,0:T(8,128)} fusion(bf16[128,512]{1,0:T(8,128)(2,1)S(1)} %copy-done.3, f32[128,16384]{1,0:T(8,128)} %get-tuple-element.15, f32[128]{0:T(128)S(1)} %log.7, s32[128]{0:T(128)S(1)} %iota_add_fusion), kind=kOutput, calls=%fused_computation.31 | convolution fusion | flops 2155872256 | bytes 42075136 | tf_op jit(solution)/shard_map/dot_general | solution.py:74
  277.9 0.1 convert_reduce_fusion
  278.1 66.8 %all-reduce.2 = f32[512]{0:T(512)S(1)} all-reduce(f32[512]{0:T(512)S(1)} %convert_reduce_fusion), channel_id=4, replica_groups=mesh['dp'=32,'grp'=4] {'dp','grp'}, use_global_device_ids=true, to_apply=%region_6.7.clone | all-reduce | flops 512 | bytes 4096
  344.8 0.2 dynamic-slice_dynamic-update-slice_fusion
  345.0 66.8 %all-reduce = f32[512]{0:T(512)S(1)} all-reduce(f32[512]{0:T(512)S(1)} %dynamic-slice_dynamic-update-slice_fusion), channel_id=1, replica_groups=mesh['dp'=32,'grp'=4] {'dp','grp'}, use_global_device_ids=true, to_apply=%add | all-reduce | flops 512 | bytes 4096
  411.7 0.2 fusion.6
  412.0 1.7 reshape.28
  413.6 596.1 %reduce-scatter.5.cloned.1.call-done = f32[128,512]{1,0:T(8,128)} async-done(((f32[16384,512]{1,0:T(8,128)}), f32[128,512]{1,0:T(8,128)}) %reduce-scatter.5.cloned.1.call-update) | async-done | bytes 262160 | tf_op jit(solution)/shard_map/reduce_scatter | solution.py:73
  1009.7 11.0 fusion.3
  1020.7 0.7 multiply_reduce_fusion
  1021.3 0.1 multiply_convert_fusion
  1021.5 0.5 convolution_bitcast_fusion
  1022.0 1.9 copy.10
  1023.9 1.3 constant_dynamic-slice_fusion
  1025.2 634.0 %reduce-scatter.7.cloned.1.call-done = f32[8,512]{1,0:T(8,128)} async-done(((f32[1024,512]{1,0:T(8,128)}), f32[8,512]{1,0:T(8,128)}) %reduce-scatter.7.cloned.1.call-update) | async-done | bytes 16400
  (26 shorter events, 0.4 us)
Async XLA Ops:
  7.2 1.2 copy-start
  7.2 154.8 %all-reduce.5.cloned.1.call-start = ((), (), s32[]{:S(2)}) async-start(), calls=%async_computation.6 | async-start | bytes 2097152
  9.9 2.4 copy-start.2
  12.2 233.6 %all-gather.4.cloned.1.call-start = ((), (), s32[]{:S(2)}) async-start(), calls=%async_computation.2 | async-start | bytes 16908288 | tf_op jit(solution)/shard_map/all_gather | solution.py:32
  13.0 399.0 %all-gather.6.cloned.1.call-start = ((), (), s32[]{:S(2)}) async-start(), calls=%async_computation.4 | async-start | bytes 1056768 | tf_op jit(solution)/shard_map/all_gather | solution.py:57
  163.4 97.3 %copy-start.3 = (bf16[128,512]{1,0:T(8,128)(2,1)S(1)}, bf16[128,512]{1,0:T(8,128)(2,1)}, u32[]{:S(2)}) copy-start(bf16[128,512]{1,0:T(8,128)(2,1)} %copy-done.2) | copy-start | bytes 393220
  163.4 846.3 %reduce-scatter.5.cloned.1.call-start = ((), (), s32[]{:S(2)}) async-start(), calls=%async_computation.3 | async-start | bytes 33816576 | tf_op jit(solution)/shard_map/reduce_scatter | solution.py:73
  277.9 1381.3 %reduce-scatter.7.cloned.1.call-start = ((), (), s32[]{:S(2)}) async-start(), calls=%async_computation.5 | async-start | bytes 2113536
  1009.7 11.8 copy-start.4
  1009.7 649.5 %copy-start.1 = (bf16[1024,512]{1,0:T(8,128)(2,1)S(1)}, bf16[1024,512]{1,0:T(8,128)(2,1)}, u32[]{:S(2)}) copy-start(bf16[1024,512]{1,0:T(8,128)(2,1)} %param.5) | copy-start | bytes 3145732
  1021.5 637.7 %copy-start.5 = (bf16[128,512]{1,0:T(8,128)(2,1)}, bf16[128,512]{1,0:T(8,128)(2,1)S(1)}, u32[]{:S(2)}) copy-start(bf16[128,512]{1,0:T(8,128)(2,1)S(1)} %multiply_convert_fusion) | copy-start | bytes 393220
Sparse Core Ops, SparseCore 0:
  12.8 149.1 all-reduce.4
  166.2 79.5 all-gather.3
  249.5 63.0 all-gather.5
  315.0 694.6 reduce-scatter.4
  1024.0 635.2 reduce-scatter.6
where the time goes:
time: 1670 us
  waiting for transfers between devices  1460 us (87%)
  blocking collectives  134 us (8%)
  matrix products  47.1 us (3%)
    unnamed x7, waiting for transfers between devices  784 us
    reduce_scatter x1, waiting for transfers between devices, body(): lax.psum_scatter(lax.dot_general(cols, unit_vectors_brain16, (((0,), (0,)...  596 us
    unnamed x2, blocking collectives  134 us
    all_gather x1, waiting for transfers between devices, body(): lax.all_gather(unit_vectors_brain16, ('dp', 'grp'), axis=0, tiled=True)  82.4 us
  transfers between devices with their start and end apart: 5, of which 4 were waited for; matrix products, arithmetic and copies ran while one was open for 2% of the time, Pallas kernels for 0%

commit v1 on v0

v1 whole, which is shorter than its diff:
```python
import jax
import jax.numpy as jnp
from jax import lax
from jax.experimental import pallas as pl
from jax.experimental.pallas import tpu as pltpu
from jax.sharding import PartitionSpec as P

MESH = pl.DeviceIdType.MESH
SIDE = 4
ROWS = 128
FEATURES = 1024
WIDTH = 512
CLASSES = 512
ROW_BLOCKS = 8
COL_BLOCKS = 16
LINE = SIDE * ROWS
N_COPIES = 80
INV_SHARPNESS = 10.0
LOG2_SCALE = 14.426950408889634
F32 = jnp.float32
BF16 = jnp.bfloat16


def dot(a, b):
    return jnp.dot(a, b, preferred_element_type=F32)


def dot_nt(a, b):
    return lax.dot_general(a, b, (((1,), (1,)), ((), ())), preferred_element_type=F32)


class Copies:
    def __init__(self, send_sems, recv_sems, any_device):
        self.send_sems, self.recv_sems, self.any_device = send_sems, recv_sems, any_device
        self.used = 0
        self.started = []

    def _copy(self, src, dst, k, device):
        return pltpu.make_async_remote_copy(
            src_ref=src,
            dst_ref=dst,
            send_sem=self.send_sems.at[k],
            recv_sem=self.recv_sems.at[k],
            device_id=device,
            device_id_type=MESH,
        )

    def send(self, src, dst, device):
        k = self.used
        self.used += 1
        copy = self._copy(src, dst, k, device)
        copy.start()
        self.started.append(copy)
        return k

    def arrived(self, dst, k):
        self._copy(dst, dst, k, self.any_device).wait_recv()

    def finish(self):
        for copy in self.started:
            copy.wait_send()


def kernel(
    feat,
    wgt,
    lab,
    slots,
    pg_out,
    wg_out,
    own_out,
    ucol,
    urow,
    unit_s,
    inv_s,
    feat_t,
    e,
    lcol,
    lrow,
    rlab,
    racc,
    rcnt,
    rinv,
    pinv,
    cinv,
    csum,
    cz1,
    cz2,
    trow,
    tz1,
    tz2,
    mu,
    osib,
    orecv,
    zsend,
    zrecv,
    g_sib,
    g_sib_recv,
    g_own,
    g_zsend,
    g_zrecv,
    g_xsend,
    g_xrecv,
    g_ysend,
    g_yrecv,
    s_part,
    s_recv,
    s_zrecv,
    send_sems,
    recv_sems,
):
    dp = lax.axis_index("dp")
    y = lax.axis_index("grp")
    c = lax.rem(dp, 2)
    x = lax.rem(lax.div(dp, 2), SIDE)
    z = lax.div(dp, 2 * SIDE)
    other = 1 - c
    p = other * x + c * y
    q = other * y + c * x

    def ring(v, o):
        return lax.rem(v + o, SIDE)

    def at(z_, x_, c_, y_):
        return ((z_ * SIDE + x_) * 2 + c_, y_)

    def at_pq(p_, q_):
        return at(z, other * p_ + c * q_, c, other * q_ + c * p_)

    sib = at(z, x, other, y)
    p_dev = [None] + [at_pq(ring(p, o), q) for o in (1, 2, 3)]
    q_dev = [None] + [at_pq(p, ring(q, o)) for o in (1, 2, 3)]
    z_dev = [None] + [at(ring(z, o), x, c, y) for o in (1, 2, 3)]
    x_dev = [None] + [at(z, ring(x, o), c, y) for o in (1, 2, 3)]
    y_dev = [None] + [at(z, x, c, ring(y, o)) for o in (1, 2, 3)]
    peers = [sib] + z_dev[1:] + x_dev[1:] + y_dev[1:]

    barrier = pltpu.get_barrier_semaphore()
    for peer in peers:
        pl.semaphore_signal(barrier, inc=1, device_id=peer, device_id_type=MESH)

    cp = Copies(send_sems, recv_sems, sib)
    my_col = q * SIDE + p
    my_row = c * SIDE + z

    projected = dot(feat[...], wgt[...])
    inv_norm = lax.rsqrt(jnp.sum(projected * projected, axis=1, keepdims=True) + 1e-06)
    unit = projected * inv_norm
    unit_s[...] = unit
    inv_s[...] = inv_norm
    u16 = unit.astype(BF16)
    ucol[my_col] = u16
    urow[my_row] = u16
    my_lab = lab[...].astype(F32)
    lcol[my_col] = my_lab
    lrow[my_row] = my_lab

    pl.semaphore_wait(barrier, len(peers))

    lab_p = [cp.send(lcol.at[my_col], lcol.at[my_col], p_dev[o]) for o in (1, 2, 3)]
    lab_z = [cp.send(lrow.at[my_row], lrow.at[my_row], z_dev[o]) for o in (1, 2, 3)]

    def whole(ref, slot):
        return ref.at[slot]

    def low(ref, slot):
        return ref.at[slot, pl.ds(0, ROWS // 2)]

    def high(ref, slot):
        return ref.at[slot, pl.ds(ROWS // 2, ROWS // 2)]

    def ring_send(ref, slot, devs):
        return [cp.send(whole(ref, slot), whole(ref, slot), devs[o]) for o in (1, 3)]

    def ring_pass_up(ref, ids, slot, devs):
        cp.arrived(whole(ref, slot), ids[0])
        return cp.send(low(ref, slot), low(ref, slot), devs[1])

    def ring_pass_down(ref, ids, slot, devs):
        cp.arrived(whole(ref, slot), ids[1])
        return cp.send(high(ref, slot), high(ref, slot), devs[3])

    def ring_far(ref, up, down, slot):
        cp.arrived(low(ref, slot), up)
        cp.arrived(high(ref, slot), down)

    def col(o_p, o_q):
        return ring(q, o_q) * SIDE + ring(p, o_p)

    def row(o_z):
        return c * SIDE + ring(z, o_z)

    def row_sib(o_z):
        return other * SIDE + ring(z, o_z)

    p_ids = ring_send(ucol, my_col, p_dev)
    z_ids = ring_send(urow, my_row, z_dev)
    q_ids = {0: ring_send(ucol, my_col, q_dev)}
    sib_ids = {0: cp.send(urow.at[my_row], urow.at[my_row], sib)}

    for o in (1, 2, 3):
        cp.arrived(lcol.at[col(SIDE - o, 0)], lab_p[o - 1])
        cp.arrived(lrow.at[row(SIDE - o)], lab_z[o - 1])
    my_line = lcol.at[pl.ds(q * SIDE, SIDE)]
    lab_q = [cp.send(my_line, my_line, q_dev[o]) for o in (1, 2, 3)]
    my_set = lrow.at[pl.ds(c * SIDE, SIDE)]
    lab_s = cp.send(my_set, my_set, sib)

    p_up = ring_pass_up(ucol, p_ids, col(3, 0), p_dev)
    q_ids[3] = ring_send(ucol, col(3, 0), q_dev)
    p_down = ring_pass_down(ucol, p_ids, col(1, 0), p_dev)
    q_ids[1] = ring_send(ucol, col(1, 0), q_dev)
    z_up = ring_pass_up(urow, z_ids, row(3), z_dev)
    sib_ids[3] = cp.send(urow.at[row(3)], urow.at[row(3)], sib)
    z_down = ring_pass_down(urow, z_ids, row(1), z_dev)
    sib_ids[1] = cp.send(urow.at[row(1)], urow.at[row(1)], sib)

    for o in (1, 2, 3):
        line = lcol.at[pl.ds(ring(q, SIDE - o) * SIDE, SIDE)]
        cp.arrived(line, lab_q[o - 1])
    cp.arrived(lrow.at[pl.ds(other * SIDE, SIDE)], lab_s)

    ring_far(ucol, p_up, p_down, col(2, 0))
    q_ids[2] = ring_send(ucol, col(2, 0), q_dev)
    ring_far(urow, z_up, z_down, row(2))
    sib_ids[2] = cp.send(urow.at[row(2)], urow.at[row(2)], sib)

    q_up, q_down = {}, {}

    def q_pass(o_p):
        q_up[o_p] = ring_pass_up(ucol, q_ids[o_p], col(o_p, 3), q_dev)
        q_down[o_p] = ring_pass_down(ucol, q_ids[o_p], col(o_p, 1), q_dev)

    q_pass(0)

    lane = lax.broadcasted_iota(jnp.int32, (ROWS, ROWS), 1)

    def turned(block):
        pad = jnp.zeros((ROWS - block.shape[0], ROWS), F32)
        return jnp.transpose(jnp.concatenate([block, pad], axis=0))

    lab_t = turned(jnp.concatenate([lrow[k] for k in range(ROW_BLOCKS)], axis=0))
    for k in range(ROW_BLOCKS):
        rlab[k * ROWS : (k + 1) * ROWS, :] = lab_t[:, k : k + 1]

    def count_block(k, carry):
        rows = pl.ds(pl.multiple_of(k * ROWS, ROWS), ROWS)
        mine = rlab[rows, :]
        total = jnp.zeros((ROWS, ROWS), F32)
        for j in range(COL_BLOCKS):
            total = total + jnp.where(mine == lcol[j], 1.0, 0.0)
        rcnt[rows, :] = jnp.sum(total, axis=1, keepdims=True)
        racc[rows, :] = jnp.zeros((ROWS, ROWS), F32)
        return carry

    lax.fori_loop(0, ROW_BLOCKS, count_block, 0)

    q_pass(3)
    q_pass(1)

    for o in (0, 3, 1, 2):
        cp.arrived(urow.at[row_sib(o)], sib_ids[o])

    TILE = 256

    def line_tiles(q_, first, last, own_line, sums):
        keys = ucol[pl.ds(q_ * SIDE, SIDE)].reshape(LINE, WIDTH)
        row_base = my_row * ROWS
        col_base = p * ROWS

        def tile(r, sums):
            rows = pl.ds(pl.multiple_of(r * TILE, TILE), TILE)
            queries = urow[pl.ds(r * 2, 2)].reshape(TILE, WIDTH)
            value = jnp.exp2(dot_nt(queries, keys) * LOG2_SCALE)
            if own_line:
                i = lax.broadcasted_iota(jnp.int32, (TILE, LINE), 0) + (r * TILE - row_base)
                j = lax.broadcasted_iota(jnp.int32, (TILE, LINE), 1) - col_base
                value = jnp.where((i == j) & (j >= 0) & (j < ROWS), 0.0, value)
            e[q_, rows, :] = value
            racc[rows, :] += (
                value[:, 0:ROWS]
                + value[:, ROWS : 2 * ROWS]
                + value[:, 2 * ROWS : 3 * ROWS]
                + value[:, 3 * ROWS : 4 * ROWS]
            )
            return sums + jnp.sum(value.reshape(TILE // 8, 8, LINE), axis=0)

        return lax.fori_loop(first, last, tile, sums)

    no_sums = jnp.zeros((8, LINE), F32)

    def put_sums(q_, sums):
        total = jnp.sum(sums, axis=0, keepdims=True)
        for k in range(SIDE):
            csum[q_ * SIDE + k] = total[:, k * ROWS : (k + 1) * ROWS]

    sums = line_tiles(q, 0, 2, True, no_sums)
    q_pass(2)
    put_sums(q, line_tiles(q, 2, 4, True, sums))
    for o in (3, 1):
        put_sums(ring(q, o), line_tiles(ring(q, o), 0, 4, False, no_sums))
    feat_t[...] = jnp.transpose(feat[...]).reshape(COL_BLOCKS, 2, 32, ROWS)
    for o_p in (0, 3, 1, 2):
        ring_far(ucol, q_up[o_p], q_down[o_p], col(o_p, 2))
    put_sums(ring(q, 2), line_tiles(ring(q, 2), 0, 4, False, no_sums))

    table = jnp.zeros((ROWS, ROWS), F32)
    for k in range(ROW_BLOCKS):
        rows = slice(k * ROWS, (k + 1) * ROWS)
        table = jnp.where(lane == k, jnp.sum(racc[rows, :], axis=1, keepdims=True), table)
        table = jnp.where(lane == ROW_BLOCKS + k, rcnt[rows, :], table)
    trow[0] = jnp.transpose(table)[0 : 2 * ROW_BLOCKS, :]
    t_ids = [cp.send(trow.at[0], tz1.at[o - 1], z_dev[o]) for o in (1, 2, 3)]
    c_ids = [cp.send(csum, cz1.at[o - 1], p_dev[o]) for o in (1, 2, 3)]

    lab_lanes = jnp.concatenate([lcol[j] for j in range(COL_BLOCKS)], axis=1)

    def all_keys():
        return ucol[...].reshape(COL_BLOCKS * ROWS, WIDTH)

    def class_tile(r, carry):
        rows = pl.ds(pl.multiple_of(r * TILE, TILE), TILE)
        same = jnp.where(rlab[rows, :] == lab_lanes, 1.0, 0.0).astype(BF16)
        mu[rows, :] = dot(same, all_keys())
        return carry

    lax.fori_loop(0, 2, class_tile, 0)

    for o in (1, 2, 3):
        cp.arrived(tz1.at[o - 1], t_ids[o - 1])
        cp.arrived(cz1.at[o - 1], c_ids[o - 1])
    trow[1] = trow[0] + tz1[0] + tz1[1] + tz1[2]
    cz2[3] = csum[...] + cz1[0] + cz1[1] + cz1[2]
    t_id2 = cp.send(trow.at[1], tz2, sib)
    c_ids2 = [cp.send(cz2.at[3], cz2.at[o - 1], q_dev[o]) for o in (1, 2, 3)]

    lax.fori_loop(2, 4, class_tile, 0)

    rho = lax.broadcasted_iota(jnp.int32, (8 * ROW_BLOCKS, 1), 0)
    block, k_slot = rho // 8, rho % 8
    owner = (((block % SIDE) * SIDE + x) * 2 + block // SIDE) * SIDE + y
    wanted = jnp.where(k_slot < 4, owner * 4 + k_slot, -1)
    class_of = jnp.zeros((8 * ROW_BLOCKS, ROWS), F32)
    lane_row = lax.broadcasted_iota(jnp.int32, (8 * ROW_BLOCKS, ROWS), 1)
    for j in range(CLASSES // ROWS):
        hit = slots[j : j + 1, :] == wanted
        class_of = class_of + jnp.where(hit, (lane_row + (j * ROWS + 1)).astype(F32), 0.0)
    class_of = jnp.sum(class_of, axis=1, keepdims=True) - 1.0
    member = jnp.where(class_of == lab_lanes, 1.0, 0.0).astype(BF16)
    s_part[...] = dot(member, all_keys()).reshape(2, SIDE, 8, WIDTH)
    s_id = cp.send(s_part.at[other], s_recv, sib)

    cp.arrived(tz2, t_id2)
    totals = trow[1] + tz2[...]
    first = lax.broadcasted_iota(jnp.int32, (2 * ROW_BLOCKS, ROWS), 0) < ROW_BLOCKS
    scales = turned(1.0 / jnp.where(first, totals, jnp.maximum(totals - 1.0, 1.0)))
    for k in range(ROW_BLOCKS):
        rows = slice(k * ROWS, (k + 1) * ROWS)
        rinv[rows, :] = scales[:, k : k + 1]
        pinv[rows, :] = 2.0 * scales[:, ROW_BLOCKS + k : ROW_BLOCKS + k + 1]
    for o in (1, 2, 3):
        cp.arrived(cz2.at[o - 1], c_ids2[o - 1])
    cinv[...] = 1.0 / (cz2[0] + cz2[1] + cz2[2] + cz2[3])
    cinv_lines = [
        jnp.concatenate([cinv[l * SIDE + k] for k in range(SIDE)], axis=1) for l in range(SIDE)
    ]

    def gradient(rows):
        scale = rinv[rows, :]
        weights = jnp.concatenate(
            [(e[l, rows, :] * (scale + cinv_lines[l])).astype(BF16) for l in range(SIDE)], axis=1
        )
        return dot(weights, all_keys()) - pinv[rows, :] * mu[rows, :]

    o_ids = []
    for h in range(2):
        rows = pl.ds(pl.multiple_of(other * LINE + h * TILE, TILE), TILE)
        half = pl.ds(h * TILE, TILE)
        osib[half, :] = gradient(rows)
        o_ids.append(cp.send(osib.at[half], orecv.at[half], sib))

    cp.arrived(s_recv, s_id)
    s_recv[...] = s_recv[...] + s_part[c]
    s_ids = [cp.send(s_recv.at[ring(z, o)], s_zrecv.at[o - 1], z_dev[o]) for o in (1, 2, 3)]

    o_zids = {}
    for n, o in enumerate((2, 1, 3, 0)):
        z_ = ring(z, o)
        rows = pl.ds(pl.multiple_of((c * SIDE + z_) * ROWS, ROWS), ROWS)
        part = gradient(rows)
        if n == 0:
            for h in range(2):
                half = pl.ds(h * TILE, TILE)
                cp.arrived(orecv.at[half], o_ids[h])
        there = pl.ds(pl.multiple_of(z_ * ROWS, ROWS), ROWS)
        part = part + orecv[there, :]
        if o:
            zsend[o - 1] = part.astype(BF16)
            o_zids[o] = cp.send(zsend.at[o - 1], zrecv.at[o - 1], z_dev[o])
    my_rows = pl.ds(pl.multiple_of(my_row * ROWS, ROWS), ROWS)
    part = part + pinv[my_rows, :] * urow[my_row].astype(F32)
    for o in (1, 2, 3):
        cp.arrived(s_zrecv.at[o - 1], s_ids[o - 1])
    own_out[...] = (s_recv[z] + s_zrecv[0] + s_zrecv[1] + s_zrecv[2])[0:4, :]
    for o in (1, 3, 2):
        cp.arrived(zrecv.at[o - 1], o_zids[o])
        part = part + zrecv[o - 1].astype(F32)
    part = part * INV_SHARPNESS
    unit = unit_s[...]
    radial = jnp.sum(unit * part, axis=1, keepdims=True)
    pg = (inv_s[...] * (part - unit * radial)).astype(BF16)
    pg_out[...] = pg

    g_sib[...] = dot(feat_t[:, other].reshape(LINE, ROWS), pg).reshape(g_sib.shape)
    g_id = cp.send(g_sib, g_sib_recv, sib)
    mine = dot(feat_t[:, c].reshape(LINE, ROWS), pg).reshape(COL_BLOCKS, 32, WIDTH)
    g_own[...] = mine
    cp.arrived(g_sib_recv, g_id)

    def z_part(z_):
        runs = pl.ds(z_ * SIDE, SIDE)
        return g_own[runs] + g_sib_recv[runs]

    ids = {}
    for o in (2, 1, 3):
        g_zsend[o - 1] = z_part(ring(z, o)).astype(BF16)
        ids[o] = cp.send(g_zsend.at[o - 1], g_zrecv.at[o - 1], z_dev[o])
    z_total = z_part(z)
    for o in (1, 3, 2):
        cp.arrived(g_zrecv.at[o - 1], ids[o])
    g_own[pl.ds(0, SIDE)] = (
        z_total
        + g_zrecv[0].astype(F32)
        + g_zrecv[1].astype(F32)
        + g_zrecv[2].astype(F32)
    )
    for o in (2, 1, 3):
        g_xsend[o - 1] = g_own[ring(x, o)]
        ids[o] = cp.send(g_xsend.at[o - 1], g_xrecv.at[o - 1], x_dev[o])
    part = g_own[x]
    for o in (1, 3, 2):
        cp.arrived(g_xrecv.at[o - 1], ids[o])
        part = part + g_xrecv[o - 1]
    g_ysend[...] = part.reshape(SIDE, 8, WIDTH)
    for o in (2, 1, 3):
        ids[o] = cp.send(g_ysend.at[ring(y, o)], g_yrecv.at[o - 1], y_dev[o])
    part = g_ysend[y]
    for o in (1, 3, 2):
        cp.arrived(g_yrecv.at[o - 1], ids[o])
        part = part + g_yrecv[o - 1]
    wg_out[...] = part

    cp.finish()


def body(features, proj_weight, labels, owner_slot):
    vmem = pl.BlockSpec(memory_space=pltpu.VMEM)
    rows_all = ROW_BLOCKS * ROWS
    scratch = [
        pltpu.VMEM((COL_BLOCKS, ROWS, WIDTH), BF16),
        pltpu.VMEM((ROW_BLOCKS, ROWS, WIDTH), BF16),
        pltpu.VMEM((ROWS, WIDTH), F32),
        pltpu.VMEM((ROWS, 1), F32),
        pltpu.VMEM((COL_BLOCKS, 2, 32, ROWS), BF16),
        pltpu.VMEM((SIDE, rows_all, LINE), F32),
        pltpu.VMEM((COL_BLOCKS, 1, ROWS), F32),
        pltpu.VMEM((ROW_BLOCKS, 1, ROWS), F32),
        pltpu.VMEM((rows_all, 1), F32),
        pltpu.VMEM((rows_all, ROWS), F32),
        pltpu.VMEM((rows_all, 1), F32),
        pltpu.VMEM((rows_all, 1), F32),
        pltpu.VMEM((rows_all, 1), F32),
        pltpu.VMEM((COL_BLOCKS, 1, ROWS), F32),
        pltpu.VMEM((COL_BLOCKS, 1, ROWS), F32),
        pltpu.VMEM((3, COL_BLOCKS, 1, ROWS), F32),
        pltpu.VMEM((4, COL_BLOCKS, 1, ROWS), F32),
        pltpu.VMEM((2, 2 * ROW_BLOCKS, ROWS), F32),
        pltpu.VMEM((3, 2 * ROW_BLOCKS, ROWS), F32),
        pltpu.VMEM((2 * ROW_BLOCKS, ROWS), F32),
        pltpu.VMEM((rows_all, WIDTH), F32),
        pltpu.VMEM((LINE, WIDTH), F32),
        pltpu.VMEM((LINE, WIDTH), F32),
        pltpu.VMEM((3, ROWS, WIDTH), BF16),
        pltpu.VMEM((3, ROWS, WIDTH), BF16),
        pltpu.VMEM((COL_BLOCKS, 32, WIDTH), F32),
        pltpu.VMEM((COL_BLOCKS, 32, WIDTH), F32),
        pltpu.VMEM((COL_BLOCKS, 32, WIDTH), F32),
        pltpu.VMEM((3, SIDE, 32, WIDTH), BF16),
        pltpu.VMEM((3, SIDE, 32, WIDTH), BF16),
        pltpu.VMEM((3, 32, WIDTH), F32),
        pltpu.VMEM((3, 32, WIDTH), F32),
        pltpu.VMEM((SIDE, 8, WIDTH), F32),
        pltpu.VMEM((3, 8, WIDTH), F32),
        pltpu.VMEM((2, SIDE, 8, WIDTH), F32),
        pltpu.VMEM((SIDE, 8, WIDTH), F32),
        pltpu.VMEM((3, 8, WIDTH), F32),
        pltpu.SemaphoreType.DMA((N_COPIES,)),
        pltpu.SemaphoreType.DMA((N_COPIES,)),
    ]
    return pl.pallas_call(
        kernel,
        out_shape=(
            jax.ShapeDtypeStruct((ROWS, WIDTH), BF16),
            jax.ShapeDtypeStruct((8, WIDTH), F32),
            jax.ShapeDtypeStruct((4, WIDTH), F32),
        ),
        in_specs=[vmem] * 4,
        out_specs=(vmem,) * 3,
        scratch_shapes=scratch,
        compiler_params=pltpu.CompilerParams(
            collective_id=0, has_side_effects=True, vmem_limit_bytes=56 * 1024 * 1024
        ),
        name="contrastive",
    )(features, proj_weight, labels.reshape(1, ROWS), owner_slot.reshape(CLASSES // ROWS, ROWS))


def solution(mesh):
    in_specs = (P(("dp", "grp"), None), P(), P(("dp", "grp")), P())
    out_specs = (P(("dp", "grp"), None), P(("dp", "grp"), None), P(("dp", "grp"), None))
    return jax.shard_map(body, mesh=mesh, in_specs=in_specs, out_specs=out_specs, check_vma=False)
```

time: 1670 us -> 71.3 us (0.04)
  waiting for transfers between devices: 1460 us -> 0 us
  blocking collectives: 134 us -> 0 us
  Pallas kernels: 0 us -> 67.5 us
  matrix products: 47.1 us -> 0 us
    unnamed x7 -> x0, waiting for transfers between devices: 784 us -> none
    reduce_scatter x1 -> x0, waiting for transfers between devices: 596 us -> none  [body(): lax.psum_scatter(lax.dot_general(cols, unit_vectors_brain16, (((0,), (0,)...]
    unnamed x2 -> x0, blocking collectives: 134 us -> none
    all_gather x2 -> x0, waiting for transfers between devices: 82.4 us -> none  [the longest x1 82.4 us: body(): lax.all_gather(unit_vectors_brain16, ('dp', 'grp'), axis=0, tiled=True)]
    pallas_call x0 -> x1, Pallas kernels: none -> 67.5 us  [body(): pl.pallas_call(kernel, out_shape=(jax.ShapeDtypeStruct((ROWS, WIDTH), BF1...]
    dot_general x8 -> x0, matrix products: 47.1 us -> none  [the longest x1 17.2 us: body(): lax.dot_general(cols, unit_vectors_brain16, (((0,), (0,)), ((), ())), pre...]
  transfers between devices with their start and end apart: 5 -> 0, of which waited for: 4 -> 0; matrix products, arithmetic and copies ran while one was open for 2% -> 0% of each run, Pallas kernels for 0% -> 0%
where the time goes in v1:
time: 71.3 us; the launch traced here: 71 us
  Pallas kernels  67.5 us (95%)
  local copies, waits for them, and re-layouts  2.88 us (4%)
    pallas_call x1, Pallas kernels, body(): pl.pallas_call(kernel, out_shape=(jax.ShapeDtypeStruct((ROWS, WIDTH), BF1...  67.5 us
    unnamed x7, local copies, waits for them, and re-layouts  2.88 us

profile of v1, /device:TPU:0, one launch (start us, length us, event | category | flops | bytes accessed | tf_op | source)
XLA Modules:
  0.0 71.0 jit_solution(1673877523507943259)
XLA Ops:
  0.6 67.5 %contrastive.1 = (bf16[128,512]{1,0:T(8,128)(2,1)}, f32[8,512]{1,0:T(8,128)}, f32[4,512]{1,0:T(4,128)}) custom-call(bf16[128,1024]{1,0:T(8,128)(2,1)} %feat.1, bf16[1024,512]{1,0:T(8,128)(2,1)} %wgt.1, s32[1,128]{1,0:T(1,128)} %bitcast.3, s32[4,128]{1,0:T(4,128)} %bitcast.2), custom_call_target="tpu_custom_call" | custom-call | tf_op jit(solution)/shard_map/contrastive/pallas_call | solution.py:500
  68.1 0.0 copy-start
  68.1 1.6 %copy.10 = bf16[128,512]{1,0:T(8,128)(2,1)} copy(bf16[128,512]{1,0:T(8,128)(2,1)} %get-tuple-element.6) | data formatting | bytes 262144
  69.7 0.0 copy-done
  69.7 0.0 copy-start.1
  69.7 0.6 copy.11
  70.3 0.1 copy-done.1
  70.4 0.6 copy.12
Async XLA Ops:
  68.1 1.6 %copy-start = (f32[8,512]{1,0:T(8,128)S(1)}, f32[8,512]{1,0:T(8,128)}, u32[]{:S(2)}) copy-start(f32[8,512]{1,0:T(8,128)} %get-tuple-element.7) | copy-start | bytes 49156
  69.7 0.7 copy-start.1

commit v2 on v1

v2 whole, which is shorter than its diff:
```python
import jax
import jax.numpy as jnp
from jax import lax
from jax.experimental import pallas as pl
from jax.experimental.pallas import tpu as pltpu
from jax.sharding import PartitionSpec as P

MESH = pl.DeviceIdType.MESH
SIDE = 4
ROWS = 128
FEATURES = 1024
WIDTH = 512
CLASSES = 512
ROW_BLOCKS = 8
COL_BLOCKS = 16
LINE = SIDE * ROWS
N_COPIES = 120
RING = (1, 3, 2)
PLANE = tuple(sorted(((a, b) for a in range(4) for b in range(4) if a or b), key=lambda o: -(min(o[0], 4 - o[0]) + min(o[1], 4 - o[1]))))
INV_SHARPNESS = 10.0
LOG2_SCALE = 14.426950408889634
F32 = jnp.float32
BF16 = jnp.bfloat16


def dot(a, b):
    return jnp.dot(a, b, preferred_element_type=F32)


def dot_nt(a, b):
    return lax.dot_general(a, b, (((1,), (1,)), ((), ())), preferred_element_type=F32)


class Copies:
    def __init__(self, send_sems, recv_sems, any_device):
        self.send_sems, self.recv_sems, self.any_device = send_sems, recv_sems, any_device
        self.used = 0
        self.started = []

    def _copy(self, src, dst, k, device):
        return pltpu.make_async_remote_copy(
            src_ref=src,
            dst_ref=dst,
            send_sem=self.send_sems.at[k],
            recv_sem=self.recv_sems.at[k],
            device_id=device,
            device_id_type=MESH,
        )

    def send(self, src, dst, device):
        k = self.used
        self.used += 1
        copy = self._copy(src, dst, k, device)
        copy.start()
        self.started.append(copy)
        return k

    def arrived(self, dst, k):
        self._copy(dst, dst, k, self.any_device).wait_recv()

    def finish(self, keep=0):
        done = len(self.started) - keep
        for copy in self.started[:done]:
            copy.wait_send()
        self.started = self.started[done:]


def kernel(
    feat_hbm,
    wgt_hbm,
    lab,
    slots,
    pg_out,
    wg_out,
    own_out,
    feat,
    wgt,
    ucol,
    urow,
    ulow,
    frow,
    feat_t,
    e,
    lcol,
    lrow,
    rlab,
    rnorm,
    racc,
    rcnt,
    rinv,
    pinv,
    csum,
    cz,
    trow,
    tz,
    mu,
    osib,
    orecv,
    obuf,
    dpart,
    g_sib,
    g_sib_recv,
    zsend,
    zrecv,
    g_own,
    g_send,
    g_recv,
    g_zsend,
    g_zrecv,
    s_part,
    s_recv,
    s_zrecv,
    send_sems,
    recv_sems,
    load_sems,
):
    dp = lax.axis_index("dp")
    y = lax.axis_index("grp")
    c = lax.rem(dp, 2)
    x = lax.rem(lax.div(dp, 2), SIDE)
    z = lax.div(dp, 2 * SIDE)
    other = 1 - c
    p = other * x + c * y
    q = other * y + c * x

    def ring(v, o):
        return lax.rem(v + o, SIDE)

    def at(z_, x_, c_, y_):
        return ((z_ * SIDE + x_) * 2 + c_, y_)

    def at_pq(p_, q_):
        return at(z, other * p_ + c * q_, c, other * q_ + c * p_)

    sib = at(z, x, other, y)
    p_dev = [None] + [at_pq(ring(p, o), q) for o in (1, 2, 3)]
    q_dev = [None] + [at_pq(p, ring(q, o)) for o in (1, 2, 3)]
    z_dev = [None] + [at(ring(z, o), x, c, y) for o in (1, 2, 3)]
    z_sib = [sib] + [at(ring(z, o), x, other, y) for o in (1, 2, 3)]
    plane = {(a, b): at(z, ring(x, a), c, ring(y, b)) for a, b in PLANE}
    peers = list(plane.values()) + z_dev[1:] + z_sib

    barrier = pltpu.get_barrier_semaphore()
    for peer in peers:
        pl.semaphore_signal(barrier, inc=1, device_id=peer, device_id_type=MESH)

    cp = Copies(send_sems, recv_sems, sib)
    my_col = q * SIDE + p
    my_row = c * SIDE + z

    loads = [
        pltpu.make_async_copy(feat_hbm, feat, load_sems.at[0]),
        pltpu.make_async_copy(wgt_hbm, wgt, load_sems.at[1]),
    ]
    for load in loads:
        load.start()
    for load in loads:
        load.wait()

    projected = dot(feat[...], wgt[...])
    inv_norm = lax.rsqrt(jnp.sum(projected * projected, axis=1, keepdims=True) + 1e-06)
    unit = projected * inv_norm
    u16 = unit.astype(BF16)
    ulow[my_row] = (unit - u16.astype(F32)).astype(BF16)
    ucol[my_col] = u16
    urow[my_row] = u16
    my_lab = lab[...].astype(F32)
    lcol[my_col] = my_lab
    inv_lanes = jnp.transpose(jnp.broadcast_to(inv_norm, (ROWS, ROWS)))[0:1, :]
    lrow[my_row] = jnp.concatenate([my_lab, inv_lanes], axis=0)

    pl.semaphore_wait(barrier, len(peers))

    lab_p = {o: cp.send(lcol.at[my_col], lcol.at[my_col], p_dev[o]) for o in RING}
    lab_z = {o: cp.send(lrow.at[my_row], lrow.at[my_row], z_dev[o]) for o in RING}

    def col(o_p, o_q):
        return ring(q, o_q) * SIDE + ring(p, o_p)

    def row(o_z):
        return c * SIDE + ring(z, o_z)

    def row_sib(o_z):
        return other * SIDE + ring(z, o_z)

    def spread(ref, slot, devs):
        return {o: cp.send(ref.at[slot], ref.at[slot], devs[o]) for o in RING}

    p_ids = spread(ucol, my_col, p_dev)
    z_ids = spread(urow, my_row, z_dev)
    q_ids = {0: spread(ucol, my_col, q_dev)}
    sib_ids = {0: cp.send(urow.at[my_row], urow.at[my_row], sib)}

    turn = jnp.transpose(feat[...].astype(F32)).reshape(SIDE, SIDE, 2, SIDE, 8, ROWS)
    for z_ in range(SIDE):
        for x_ in range(SIDE):
            for c_ in range(2):
                for y_ in range(SIDE):
                    feat_t[c_, x_, y_, z_] = turn[z_, x_, c_, y_]
    frow[my_row] = feat_t[...].reshape(FEATURES, ROWS).astype(BF16)

    for o in RING:
        cp.arrived(lcol.at[col(SIDE - o, 0)], lab_p[o])
        cp.arrived(lrow.at[row(SIDE - o)], lab_z[o])
    my_line = lcol.at[pl.ds(q * SIDE, SIDE)]
    lab_q = {o: cp.send(my_line, my_line, q_dev[o]) for o in RING}
    my_set = lrow.at[pl.ds(c * SIDE, SIDE)]
    lab_s = cp.send(my_set, my_set, sib)

    for o in RING:
        back = SIDE - o
        cp.arrived(ucol.at[col(back, 0)], p_ids[o])
        q_ids[back] = spread(ucol, col(back, 0), q_dev)
        cp.arrived(urow.at[row(back)], z_ids[o])
        sib_ids[back] = cp.send(urow.at[row(back)], urow.at[row(back)], sib)

    late_z = [(ref, spread(ref, my_row, z_dev)) for ref in (ulow, frow)]
    late_s = [(ref, {0: cp.send(ref.at[my_row], ref.at[my_row], sib)}) for ref in (ulow, frow)]

    for o in RING:
        line = lcol.at[pl.ds(ring(q, SIDE - o) * SIDE, SIDE)]
        cp.arrived(line, lab_q[o])
    cp.arrived(lrow.at[pl.ds(other * SIDE, SIDE)], lab_s)

    lane = lax.broadcasted_iota(jnp.int32, (ROWS, ROWS), 1)

    def turned(block):
        pad = jnp.zeros((ROWS - block.shape[0], ROWS), F32)
        return jnp.transpose(jnp.concatenate([block, pad], axis=0))

    lab_t = turned(jnp.concatenate([lrow[k] for k in range(ROW_BLOCKS)], axis=0))
    for k in range(ROW_BLOCKS):
        rlab[k * ROWS : (k + 1) * ROWS, :] = lab_t[:, 2 * k : 2 * k + 1]
        rnorm[k * ROWS : (k + 1) * ROWS, :] = lab_t[:, 2 * k + 1 : 2 * k + 2] * INV_SHARPNESS

    def count_block(k, carry):
        rows = pl.ds(pl.multiple_of(k * ROWS, ROWS), ROWS)
        mine = rlab[rows, :]
        total = jnp.zeros((ROWS, ROWS), F32)
        for j in range(COL_BLOCKS):
            total = total + jnp.where(mine == lcol[j], 1.0, 0.0)
        rcnt[rows, :] = jnp.sum(total, axis=1, keepdims=True)
        racc[rows, :] = jnp.zeros((ROWS, ROWS), F32)
        return carry

    lax.fori_loop(0, ROW_BLOCKS, count_block, 0)

    for o in (0, 3, 1, 2):
        cp.arrived(urow.at[row_sib(o)], sib_ids[o])

    TILE = 256

    def line_tiles(q_, first, last, own_line, sums):
        keys = ucol[pl.ds(q_ * SIDE, SIDE)].reshape(LINE, WIDTH)
        row_base = my_row * ROWS
        col_base = p * ROWS

        def tile(r, sums):
            rows = pl.ds(pl.multiple_of(r * TILE, TILE), TILE)
            queries = urow[pl.ds(r * 2, 2)].reshape(TILE, WIDTH)
            value = jnp.exp2(dot_nt(queries, keys) * LOG2_SCALE)
            if own_line:
                i = lax.broadcasted_iota(jnp.int32, (TILE, LINE), 0) + (r * TILE - row_base)
                j = lax.broadcasted_iota(jnp.int32, (TILE, LINE), 1) - col_base
                value = jnp.where((i == j) & (j >= 0) & (j < ROWS), 0.0, value)
            e[q_, rows, :] = value
            racc[rows, :] += (
                value[:, 0:ROWS]
                + value[:, ROWS : 2 * ROWS]
                + value[:, 2 * ROWS : 3 * ROWS]
                + value[:, 3 * ROWS : 4 * ROWS]
            )
            return sums + jnp.sum(value.reshape(TILE // 8, 8, LINE), axis=0)

        return lax.fori_loop(first, last, tile, sums)

    no_sums = jnp.zeros((8, LINE), F32)

    def put_sums(q_, sums):
        total = jnp.sum(sums, axis=0, keepdims=True)
        for k in range(SIDE):
            csum[pl.ds(q_ * SIDE + k, 1), :] = total[:, k * ROWS : (k + 1) * ROWS]

    put_sums(q, line_tiles(q, 0, 4, True, no_sums))
    for o in RING:
        for o_p in (0, 3, 1, 2):
            cp.arrived(ucol.at[col(o_p, SIDE - o)], q_ids[o_p][o])
        q_ = ring(q, SIDE - o)
        put_sums(q_, line_tiles(q_, 0, 4, False, no_sums))

    table = jnp.zeros((ROWS, ROWS), F32)
    for k in range(ROW_BLOCKS):
        rows = slice(k * ROWS, (k + 1) * ROWS)
        table = jnp.where(lane == k, jnp.sum(racc[rows, :], axis=1, keepdims=True), table)
        table = jnp.where(lane == ROW_BLOCKS + k, rcnt[rows, :], table)
    trow[...] = jnp.transpose(table)[0 : 2 * ROW_BLOCKS, :]
    t_ids = {}
    for o in RING:
        t_ids[o] = cp.send(trow, tz.at[o], z_dev[o])
        t_ids[4 + o] = cp.send(trow, tz.at[4 + o], z_sib[o])
    t_ids[4] = cp.send(trow, tz.at[4], sib)
    c_ids = {o: cp.send(csum, cz.at[o[0] * SIDE + o[1]], plane[o]) for o in PLANE}

    lab_lanes = jnp.concatenate([lcol[j] for j in range(COL_BLOCKS)], axis=1)

    def all_keys():
        return ucol[...].reshape(COL_BLOCKS * ROWS, WIDTH)

    def class_tile(r, carry):
        rows = pl.ds(pl.multiple_of(r * TILE, TILE), TILE)
        same = jnp.where(rlab[rows, :] == lab_lanes, 1.0, 0.0).astype(BF16)
        mu[rows, :] = dot(same, all_keys())
        return carry

    lax.fori_loop(0, 4, class_tile, 0)
    my_rows = pl.ds(pl.multiple_of(my_row * ROWS, ROWS), ROWS)
    mu[my_rows, :] = mu[my_rows, :] - urow[my_row].astype(F32)

    rho = lax.broadcasted_iota(jnp.int32, (8 * ROW_BLOCKS, 1), 0)
    block, k_slot = rho // 8, rho % 8
    owner = (((block % SIDE) * SIDE + x) * 2 + block // SIDE) * SIDE + y
    wanted = jnp.where(k_slot < 4, owner * 4 + k_slot, -1)
    class_of = jnp.zeros((8 * ROW_BLOCKS, ROWS), F32)
    lane_row = lax.broadcasted_iota(jnp.int32, (8 * ROW_BLOCKS, ROWS), 1)
    for j in range(CLASSES // ROWS):
        hit = slots[j : j + 1, :] == wanted
        class_of = class_of + jnp.where(hit, (lane_row + (j * ROWS + 1)).astype(F32), 0.0)
    class_of = jnp.sum(class_of, axis=1, keepdims=True) - 1.0
    member = jnp.where(class_of == lab_lanes, 1.0, 0.0).astype(BF16)
    s_part[...] = dot(member, all_keys()).reshape(2, SIDE, 8, WIDTH)
    s_id = cp.send(s_part.at[other], s_recv, sib)

    for (ref, z_sent), (_, s_sent) in zip(late_z, late_s):
        for o in RING:
            back = SIDE - o
            cp.arrived(ref.at[row(back)], z_sent[o])
            s_sent[back] = cp.send(ref.at[row(back)], ref.at[row(back)], sib)
    cp.finish()

    totals = trow[...]
    for o in t_ids:
        cp.arrived(tz.at[o], t_ids[o])
        totals = totals + tz[o]
    first = lax.broadcasted_iota(jnp.int32, (2 * ROW_BLOCKS, ROWS), 0) < ROW_BLOCKS
    scales = turned(1.0 / jnp.where(first, totals, jnp.maximum(totals - 1.0, 1.0)))
    for k in range(ROW_BLOCKS):
        rows = slice(k * ROWS, (k + 1) * ROWS)
        rinv[rows, :] = scales[:, k : k + 1]
        pinv[rows, :] = 2.0 * scales[:, ROW_BLOCKS + k : ROW_BLOCKS + k + 1]
    col_totals = csum[...]
    for o in PLANE:
        cp.arrived(cz.at[o[0] * SIDE + o[1]], c_ids[o])
        col_totals = col_totals + cz[o[0] * SIDE + o[1]]
    cinv = 1.0 / col_totals
    cinv_lines = [
        jnp.concatenate([cinv[l * SIDE + k : l * SIDE + k + 1, :] for k in range(SIDE)], axis=1)
        for l in range(SIDE)
    ]

    def gradient(rows):
        scale = rinv[rows, :]
        weights = jnp.concatenate(
            [(e[l, rows, :] * (scale + cinv_lines[l])).astype(BF16) for l in range(SIDE)], axis=1
        )
        return dot(weights, all_keys()) - pinv[rows, :] * mu[rows, :]

    def project(part, rows, block, count):
        high = urow[pl.ds(block, count)].astype(F32).reshape(part.shape)
        unit = high + ulow[pl.ds(block, count)].astype(F32).reshape(part.shape)
        radial = jnp.sum(unit * part, axis=1, keepdims=True)
        return (rnorm[rows, :] * (part - unit * radial)).astype(BF16)

    def late_wait(o):
        for ref, s_sent in late_s:
            cp.arrived(ref.at[row_sib(o)], s_sent[o])

    for o in range(SIDE):
        late_wait(o)

    o_ids = []
    for c_, keep in ((other, osib), (c, obuf)):
        for h in range(2):
            first_row = c_ * LINE + h * TILE
            rows = pl.ds(pl.multiple_of(first_row, TILE), TILE)
            half = pl.ds(h * TILE, TILE)
            part = gradient(rows)
            keep[half, :] = part
            if keep is osib:
                o_ids.append(cp.send(osib.at[half], orecv.at[half], sib))
            dpart[rows, :] = project(part, rows, c_ * SIDE + 2 * h, 2)

    def feats(c_, h):
        runs = pl.ds(pl.multiple_of(c_ * LINE + h * TILE, TILE), TILE)
        return jnp.concatenate([frow[k, runs, :] for k in range(ROW_BLOCKS)], axis=1)

    gs_ids = []
    for h in range(2):
        half = pl.ds(h * TILE, TILE)
        g_sib[half] = dot(feats(other, h), dpart[...])
        gs_ids.append(cp.send(g_sib.at[half], g_sib_recv.at[half], sib))
    for h in range(2):
        g_own[pl.ds(2 * h, 2)] = dot(feats(c, h), dpart[...]).reshape(2, SIDE, 4 * 8, WIDTH)

    cp.arrived(s_recv, s_id)
    s_recv[...] = s_recv[...] + s_part[c]
    s_ids = [cp.send(s_recv.at[ring(z, o)], s_zrecv.at[o - 1], z_dev[o]) for o in (1, 2, 3)]

    o_zids = {}
    for h in range(2):
        cp.arrived(orecv.at[pl.ds(h * TILE, TILE)], o_ids[h])

    def rows_of(z_):
        there = pl.ds(pl.multiple_of(z_ * ROWS, ROWS), ROWS)
        return obuf[there, :] + orecv[there, :]

    for o in (2, 1, 3):
        zsend[o - 1] = rows_of(ring(z, o)).astype(BF16)
        o_zids[o] = cp.send(zsend.at[o - 1], zrecv.at[o - 1], z_dev[o])

    for h in range(2):
        half = pl.ds(h * TILE, TILE)
        cp.arrived(g_sib_recv.at[half], gs_ids[h])
        g_own[pl.ds(2 * h, 2)] = g_own[pl.ds(2 * h, 2)] + g_sib_recv[half].reshape(
            2, SIDE, 4 * 8, WIDTH
        )
    g_ids = {}
    for o in PLANE:
        k = o[0] * SIDE + o[1]
        g_send[k] = g_own[ring(x, o[0]), ring(y, o[1])].astype(BF16)
        g_ids[o] = cp.send(g_send.at[k], g_recv.at[k], plane[o])

    for o in (1, 2, 3):
        cp.arrived(s_zrecv.at[o - 1], s_ids[o - 1])
    own_out[...] = (s_recv[z] + s_zrecv[0] + s_zrecv[1] + s_zrecv[2])[0:4, :]
    part = rows_of(z)
    for o in (1, 3, 2):
        cp.arrived(zrecv.at[o - 1], o_zids[o])
        part = part + zrecv[o - 1].astype(F32)
    pg_out[...] = project(part, my_rows, my_row, 1)

    part = g_own[x, y]
    for o in PLANE[::-1]:
        k = o[0] * SIDE + o[1]
        cp.arrived(g_recv.at[k], g_ids[o])
        part = part + g_recv[k].astype(F32)
    g_zsend[...] = part.reshape(SIDE, 8, WIDTH)
    ids = {o: cp.send(g_zsend.at[ring(z, o)], g_zrecv.at[o - 1], z_dev[o]) for o in (2, 1, 3)}
    cp.finish(3)
    part = g_zsend[z]
    for o in (1, 3, 2):
        cp.arrived(g_zrecv.at[o - 1], ids[o])
        part = part + g_zrecv[o - 1]
    wg_out[...] = part

    cp.finish()


def body(features, proj_weight, labels, owner_slot):
    vmem = pl.BlockSpec(memory_space=pltpu.VMEM)
    rows_all = ROW_BLOCKS * ROWS
    scratch = [
        pltpu.VMEM((ROWS, FEATURES), BF16),
        pltpu.VMEM((FEATURES, WIDTH), BF16),
        pltpu.VMEM((COL_BLOCKS, ROWS, WIDTH), BF16),
        pltpu.VMEM((ROW_BLOCKS, ROWS, WIDTH), BF16),
        pltpu.VMEM((ROW_BLOCKS, ROWS, WIDTH), BF16),
        pltpu.VMEM((ROW_BLOCKS, FEATURES, ROWS), BF16),
        pltpu.VMEM((2, SIDE, SIDE, SIDE, 8, ROWS), F32),
        pltpu.VMEM((SIDE, rows_all, LINE), F32),
        pltpu.VMEM((COL_BLOCKS, 1, ROWS), F32),
        pltpu.VMEM((ROW_BLOCKS, 2, ROWS), F32),
        pltpu.VMEM((rows_all, 1), F32),
        pltpu.VMEM((rows_all, 1), F32),
        pltpu.VMEM((rows_all, ROWS), F32),
        pltpu.VMEM((rows_all, 1), F32),
        pltpu.VMEM((rows_all, 1), F32),
        pltpu.VMEM((rows_all, 1), F32),
        pltpu.VMEM((COL_BLOCKS, ROWS), F32),
        pltpu.VMEM((16, COL_BLOCKS, ROWS), F32),
        pltpu.VMEM((2 * ROW_BLOCKS, ROWS), F32),
        pltpu.VMEM((8, 2 * ROW_BLOCKS, ROWS), F32),
        pltpu.VMEM((rows_all, WIDTH), F32),
        pltpu.VMEM((LINE, WIDTH), F32),
        pltpu.VMEM((LINE, WIDTH), F32),
        pltpu.VMEM((LINE, WIDTH), F32),
        pltpu.VMEM((rows_all, WIDTH), BF16),
        pltpu.VMEM((LINE, WIDTH), F32),
        pltpu.VMEM((LINE, WIDTH), F32),
        pltpu.VMEM((3, ROWS, WIDTH), BF16),
        pltpu.VMEM((3, ROWS, WIDTH), BF16),
        pltpu.VMEM((SIDE, SIDE, 4 * 8, WIDTH), F32),
        pltpu.VMEM((16, 4 * 8, WIDTH), BF16),
        pltpu.VMEM((16, 4 * 8, WIDTH), BF16),
        pltpu.VMEM((SIDE, 8, WIDTH), F32),
        pltpu.VMEM((3, 8, WIDTH), F32),
        pltpu.VMEM((2, SIDE, 8, WIDTH), F32),
        pltpu.VMEM((SIDE, 8, WIDTH), F32),
        pltpu.VMEM((3, 8, WIDTH), F32),
        pltpu.SemaphoreType.DMA((N_COPIES,)),
        pltpu.SemaphoreType.DMA((N_COPIES,)),
        pltpu.SemaphoreType.DMA((2,)),
    ]
    return pl.pallas_call(
        kernel,
        out_shape=(
            jax.ShapeDtypeStruct((ROWS, WIDTH), BF16),
            jax.ShapeDtypeStruct((8, WIDTH), F32),
            jax.ShapeDtypeStruct((4, WIDTH), F32),
        ),
        in_specs=[pl.BlockSpec(memory_space=pl.ANY)] * 2 + [vmem] * 2,
        out_specs=(vmem,) * 3,
        scratch_shapes=scratch,
        compiler_params=pltpu.CompilerParams(
            collective_id=0, has_side_effects=True, vmem_limit_bytes=56 * 1024 * 1024
        ),
        name="contrastive",
    )(features, proj_weight, labels.reshape(1, ROWS), owner_slot.reshape(CLASSES // ROWS, ROWS))


def solution(mesh):
    in_specs = (P(("dp", "grp"), None), P(), P(("dp", "grp")), P())
    out_specs = (P(("dp", "grp"), None), P(("dp", "grp"), None), P(("dp", "grp"), None))
    return jax.shard_map(body, mesh=mesh, in_specs=in_specs, out_specs=out_specs, check_vma=False)
```

time: 71.3 us -> 61.7 us (0.87)
  Pallas kernels: 67.5 us -> 57.9 us
    pallas_call x1, Pallas kernels: 67.5 us -> 57.9 us  [body(): pl.pallas_call(kernel, out_shape=(jax.ShapeDtypeStruct((ROWS, WIDTH), BF1...]
where the time goes in v2:
time: 61.7 us; the launch traced here: 61.4 us
  Pallas kernels  57.9 us (94%)
  local copies, waits for them, and re-layouts  2.88 us (5%)
  between operations  0.65 us (1%)
    pallas_call x1, Pallas kernels, body(): pl.pallas_call(kernel, out_shape=(jax.ShapeDtypeStruct((ROWS, WIDTH), BF1...  57.9 us
    unnamed x7, local copies, waits for them, and re-layouts  2.88 us

profile of v2, /device:TPU:0, one launch (start us, length us, event | category | flops | bytes accessed | tf_op | source)
XLA Modules:
  0.0 61.4 jit_solution(1367968065424493142)
XLA Ops:
  0.6 57.9 %contrastive.1 = (bf16[128,512]{1,0:T(8,128)(2,1)}, f32[8,512]{1,0:T(8,128)}, f32[4,512]{1,0:T(4,128)}) custom-call(bf16[128,1024]{1,0:T(8,128)(2,1)} %feat_hbm.1, bf16[1024,512]{1,0:T(8,128)(2,1)} %wgt_hbm.1, s32[1,128]{1,0:T(1,128)} %bitcast.3, s32[4,128]{1,0:T(4,128)} %bitcast.2), custom_call_target="tpu_custom_call" | custom-call | tf_op jit(solution)/shard_map/contrastive/pallas_call | solution.py:503
  58.5 0.0 copy-start
  58.5 1.6 %copy.10 = bf16[128,512]{1,0:T(8,128)(2,1)} copy(bf16[128,512]{1,0:T(8,128)(2,1)} %get-tuple-element.6) | data formatting | bytes 262144
  60.1 0.0 copy-done
  60.1 0.0 copy-start.1
  60.1 0.6 copy.11
  60.7 0.1 copy-done.1
  60.8 0.6 copy.12
Async XLA Ops:
  58.5 1.6 %copy-start = (f32[8,512]{1,0:T(8,128)S(1)}, f32[8,512]{1,0:T(8,128)}, u32[]{:S(2)}) copy-start(f32[8,512]{1,0:T(8,128)} %get-tuple-element.7) | copy-start | bytes 49156
  60.1 0.7 %copy-start.1 = (f32[4,512]{1,0:T(4,128)S(1)}, f32[4,512]{1,0:T(4,128)}, u32[]{:S(2)}) copy-start(f32[4,512]{1,0:T(4,128)} %get-tuple-element.8) | copy-start | bytes 24580

commit v3 on v2

--- a/solution.py
+++ b/solution.py
@@ -183,13 +183,18 @@
     def row_sib(o_z):
         return other * SIDE + ring(z, o_z)
 
-    def spread(ref, slot, devs):
-        return {o: cp.send(ref.at[slot], ref.at[slot], devs[o]) for o in RING}
-
-    p_ids = spread(ucol, my_col, p_dev)
+    def spread(ref, slot, devs, offsets=RING):
+        return {o: cp.send(ref.at[slot], ref.at[slot], devs[o]) for o in offsets}
+
+    p_ids = spread(ucol, my_col, p_dev, (1, 3))
+    first_sent, cp.started = cp.started[-2:], cp.started[:-2]
     z_ids = spread(urow, my_row, z_dev)
-    q_ids = {0: spread(ucol, my_col, q_dev)}
     sib_ids = {0: cp.send(urow.at[my_row], urow.at[my_row], sib)}
+    for copy in first_sent:
+        copy.wait_send()
+    p_ids.update(spread(ucol, my_col, p_dev, (2,)))
+    q_ids = {0: spread(ucol, my_col, q_dev, (1, 3))}
+    late_z = [(ulow, spread(ulow, my_row, z_dev))]
 
     turn = jnp.transpose(feat[...].astype(F32)).reshape(SIDE, SIDE, 2, SIDE, 8, ROWS)
     for z_ in range(SIDE):
@@ -198,6 +203,7 @@
                 for y_ in range(SIDE):
                     feat_t[c_, x_, y_, z_] = turn[z_, x_, c_, y_]
     frow[my_row] = feat_t[...].reshape(FEATURES, ROWS).astype(BF16)
+    late_z.append((frow, spread(frow, my_row, z_dev)))
 
     for o in RING:
         cp.arrived(lcol.at[col(SIDE - o, 0)], lab_p[o])
@@ -207,14 +213,20 @@
     my_set = lrow.at[pl.ds(c * SIDE, SIDE)]
     lab_s = cp.send(my_set, my_set, sib)
 
+    for o in (1, 3):
+        back = SIDE - o
+        cp.arrived(ucol.at[col(back, 0)], p_ids[o])
+        q_ids[back] = spread(ucol, col(back, 0), q_dev, (1, 3))
+    q_ids[0].update(spread(ucol, my_col, q_dev, (2,)))
+    for back in (3, 1):
+        q_ids[back].update(spread(ucol, col(back, 0), q_dev, (2,)))
+    cp.arrived(ucol.at[col(2, 0)], p_ids[2])
+    q_ids[2] = spread(ucol, col(2, 0), q_dev)
     for o in RING:
         back = SIDE - o
-        cp.arrived(ucol.at[col(back, 0)], p_ids[o])
-        q_ids[back] = spread(ucol, col(back, 0), q_dev)
         cp.arrived(urow.at[row(back)], z_ids[o])
         sib_ids[back] = cp.send(urow.at[row(back)], urow.at[row(back)], sib)
 
-    late_z = [(ref, spread(ref, my_row, z_dev)) for ref in (ulow, frow)]
     late_s = [(ref, {0: cp.send(ref.at[my_row], ref.at[my_row], sib)}) for ref in (ulow, frow)]
 
     for o in RING:
@@ -250,43 +262,34 @@
 
     TILE = 256
 
-    def line_tiles(q_, first, last, own_line, sums):
+    def line_tiles(q_, own_line):
         keys = ucol[pl.ds(q_ * SIDE, SIDE)].reshape(LINE, WIDTH)
-        row_base = my_row * ROWS
-        col_base = p * ROWS
-
-        def tile(r, sums):
-            rows = pl.ds(pl.multiple_of(r * TILE, TILE), TILE)
-            queries = urow[pl.ds(r * 2, 2)].reshape(TILE, WIDTH)
-            value = jnp.exp2(dot_nt(queries, keys) * LOG2_SCALE)
-            if own_line:
-                i = lax.broadcasted_iota(jnp.int32, (TILE, LINE), 0) + (r * TILE - row_base)
-                j = lax.broadcasted_iota(jnp.int32, (TILE, LINE), 1) - col_base
-                value = jnp.where((i == j) & (j >= 0) & (j < ROWS), 0.0, value)
-            e[q_, rows, :] = value
-            racc[rows, :] += (
-                value[:, 0:ROWS]
-                + value[:, ROWS : 2 * ROWS]
-                + value[:, 2 * ROWS : 3 * ROWS]
-                + value[:, 3 * ROWS : 4 * ROWS]
-            )
-            return sums + jnp.sum(value.reshape(TILE // 8, 8, LINE), axis=0)
-
-        return lax.fori_loop(first, last, tile, sums)
-
-    no_sums = jnp.zeros((8, LINE), F32)
+        queries = urow[...].reshape(ROW_BLOCKS * ROWS, WIDTH)
+        value = jnp.exp2(dot_nt(queries, keys) * LOG2_SCALE)
+        if own_line:
+            i = lax.broadcasted_iota(jnp.int32, value.shape, 0) - my_row * ROWS
+            j = lax.broadcasted_iota(jnp.int32, value.shape, 1) - p * ROWS
+            value = jnp.where((i == j) & (j >= 0) & (j < ROWS), 0.0, value)
+        e[q_] = value
+        racc[...] += (
+            value[:, 0:ROWS]
+            + value[:, ROWS : 2 * ROWS]
+            + value[:, 2 * ROWS : 3 * ROWS]
+            + value[:, 3 * ROWS : 4 * ROWS]
+        )
+        return jnp.sum(value.reshape(ROW_BLOCKS * ROWS // 8, 8, LINE), axis=0)
 
     def put_sums(q_, sums):
         total = jnp.sum(sums, axis=0, keepdims=True)
         for k in range(SIDE):
             csum[pl.ds(q_ * SIDE + k, 1), :] = total[:, k * ROWS : (k + 1) * ROWS]
 
-    put_sums(q, line_tiles(q, 0, 4, True, no_sums))
+    put_sums(q, line_tiles(q, True))
     for o in RING:
         for o_p in (0, 3, 1, 2):
             cp.arrived(ucol.at[col(o_p, SIDE - o)], q_ids[o_p][o])
         q_ = ring(q, SIDE - o)
-        put_sums(q_, line_tiles(q_, 0, 4, False, no_sums))
+        put_sums(q_, line_tiles(q_, False))
 
     table = jnp.zeros((ROWS, ROWS), F32)
     for k in range(ROW_BLOCKS):

time: 61.7 us -> 59.2 us (0.959)
  Pallas kernels: 57.9 us -> 55.5 us
    pallas_call x1, Pallas kernels: 57.9 us -> 55.5 us  [body(): pl.pallas_call(kernel, out_shape=(jax.ShapeDtypeStruct((ROWS, WIDTH), BF1...]
where the time goes in v3:
time: 59.2 us; the launch traced here: 59 us
  Pallas kernels  55.5 us (94%)
  local copies, waits for them, and re-layouts  2.88 us (5%)
  between operations  0.65 us (1%)
    pallas_call x1, Pallas kernels, body(): pl.pallas_call(kernel, out_shape=(jax.ShapeDtypeStruct((ROWS, WIDTH), BF1...  55.5 us
    unnamed x7, local copies, waits for them, and re-layouts  2.88 us

profile of v3, /device:TPU:0, one launch (start us, length us, event | category | flops | bytes accessed | tf_op | source)
XLA Modules:
  0.0 59.0 jit_solution(14817869411967723883)
XLA Ops:
  0.6 55.5 %contrastive.1 = (bf16[128,512]{1,0:T(8,128)(2,1)}, f32[8,512]{1,0:T(8,128)}, f32[4,512]{1,0:T(4,128)}) custom-call(bf16[128,1024]{1,0:T(8,128)(2,1)} %feat_hbm.1, bf16[1024,512]{1,0:T(8,128)(2,1)} %wgt_hbm.1, s32[1,128]{1,0:T(1,128)} %bitcast.3, s32[4,128]{1,0:T(4,128)} %bitcast.2), custom_call_target="tpu_custom_call" | custom-call | tf_op jit(solution)/shard_map/contrastive/pallas_call | solution.py:506
  56.1 0.0 copy-start
  56.1 1.6 %copy.10 = bf16[128,512]{1,0:T(8,128)(2,1)} copy(bf16[128,512]{1,0:T(8,128)(2,1)} %get-tuple-element.6) | data formatting | bytes 262144
  57.7 0.0 copy-done
  57.7 0.0 copy-start.1
  57.7 0.6 %copy.11 = f32[8,512]{1,0:T(8,128)} copy(f32[8,512]{1,0:T(8,128)S(1)} %copy-done) | data formatting | bytes 32768
  58.3 0.1 copy-done.1
  58.4 0.6 %copy.12 = f32[4,512]{1,0:T(4,128)} copy(f32[4,512]{1,0:T(4,128)S(1)} %copy-done.1) | data formatting | bytes 16384
Async XLA Ops:
  56.1 1.6 %copy-start = (f32[8,512]{1,0:T(8,128)S(1)}, f32[8,512]{1,0:T(8,128)}, u32[]{:S(2)}) copy-start(f32[8,512]{1,0:T(8,128)} %get-tuple-element.7) | copy-start | bytes 49156
  57.7 0.7 %copy-start.1 = (f32[4,512]{1,0:T(4,128)S(1)}, f32[4,512]{1,0:T(4,128)}, u32[]{:S(2)}) copy-start(f32[4,512]{1,0:T(4,128)} %get-tuple-element.8) | copy-start | bytes 24580

commit v4 on v3

--- a/solution.py
+++ b/solution.py
@@ -138,7 +138,7 @@
     z_dev = [None] + [at(ring(z, o), x, c, y) for o in (1, 2, 3)]
     z_sib = [sib] + [at(ring(z, o), x, other, y) for o in (1, 2, 3)]
     plane = {(a, b): at(z, ring(x, a), c, ring(y, b)) for a, b in PLANE}
-    peers = list(plane.values()) + z_dev[1:] + z_sib
+    peers = p_dev[1:] + q_dev[1:] + z_dev[1:] + [sib]
 
     barrier = pltpu.get_barrier_semaphore()
     for peer in peers:
@@ -291,6 +291,7 @@
         q_ = ring(q, SIDE - o)
         put_sums(q_, line_tiles(q_, False))
 
+    c_ids = {o: cp.send(csum, cz.at[o[0] * SIDE + o[1]], plane[o]) for o in PLANE}
     table = jnp.zeros((ROWS, ROWS), F32)
     for k in range(ROW_BLOCKS):
         rows = slice(k * ROWS, (k + 1) * ROWS)
@@ -302,7 +303,6 @@
         t_ids[o] = cp.send(trow, tz.at[o], z_dev[o])
         t_ids[4 + o] = cp.send(trow, tz.at[4 + o], z_sib[o])
     t_ids[4] = cp.send(trow, tz.at[4], sib)
-    c_ids = {o: cp.send(csum, cz.at[o[0] * SIDE + o[1]], plane[o]) for o in PLANE}
 
     lab_lanes = jnp.concatenate([lcol[j] for j in range(COL_BLOCKS)], axis=1)
 
@@ -380,17 +380,13 @@
     for o in range(SIDE):
         late_wait(o)
 
-    o_ids = []
     for c_, keep in ((other, osib), (c, obuf)):
-        for h in range(2):
-            first_row = c_ * LINE + h * TILE
-            rows = pl.ds(pl.multiple_of(first_row, TILE), TILE)
-            half = pl.ds(h * TILE, TILE)
-            part = gradient(rows)
-            keep[half, :] = part
-            if keep is osib:
-                o_ids.append(cp.send(osib.at[half], orecv.at[half], sib))
-            dpart[rows, :] = project(part, rows, c_ * SIDE + 2 * h, 2)
+        rows = pl.ds(pl.multiple_of(c_ * LINE, LINE), LINE)
+        part = gradient(rows)
+        keep[...] = part
+        if keep is osib:
+            o_id = cp.send(osib, orecv, sib)
+        dpart[rows, :] = project(part, rows, c_ * SIDE, SIDE)
 
     def feats(c_, h):
         runs = pl.ds(pl.multiple_of(c_ * LINE + h * TILE, TILE), TILE)
@@ -409,8 +405,7 @@
     s_ids = [cp.send(s_recv.at[ring(z, o)], s_zrecv.at[o - 1], z_dev[o]) for o in (1, 2, 3)]
 
     o_zids = {}
-    for h in range(2):
-        cp.arrived(orecv.at[pl.ds(h * TILE, TILE)], o_ids[h])
+    cp.arrived(orecv, o_id)
 
     def rows_of(z_):
         there = pl.ds(pl.multiple_of(z_ * ROWS, ROWS), ROWS)
@@ -421,15 +416,16 @@
         o_zids[o] = cp.send(zsend.at[o - 1], zrecv.at[o - 1], z_dev[o])
 
     for h in range(2):
-        half = pl.ds(h * TILE, TILE)
-        cp.arrived(g_sib_recv.at[half], gs_ids[h])
-        g_own[pl.ds(2 * h, 2)] = g_own[pl.ds(2 * h, 2)] + g_sib_recv[half].reshape(
-            2, SIDE, 4 * 8, WIDTH
-        )
+        cp.arrived(g_sib_recv.at[pl.ds(h * TILE, TILE)], gs_ids[h])
+
+    def g_rows(x_, y_):
+        runs = pl.ds(pl.multiple_of((x_ * SIDE + y_) * 32, 32), 32)
+        return g_own[x_, y_] + g_sib_recv[runs, :]
+
     g_ids = {}
     for o in PLANE:
         k = o[0] * SIDE + o[1]
-        g_send[k] = g_own[ring(x, o[0]), ring(y, o[1])].astype(BF16)
+        g_send[k] = g_rows(ring(x, o[0]), ring(y, o[1])).astype(BF16)
         g_ids[o] = cp.send(g_send.at[k], g_recv.at[k], plane[o])
 
     for o in (1, 2, 3):
@@ -441,7 +437,7 @@
         part = part + zrecv[o - 1].astype(F32)
     pg_out[...] = project(part, my_rows, my_row, 1)
 
-    part = g_own[x, y]
+    part = g_rows(x, y)
     for o in PLANE[::-1]:
         k = o[0] * SIDE + o[1]
         cp.arrived(g_recv.at[k], g_ids[o])
@@ -506,9 +502,9 @@
     return pl.pallas_call(
         kernel,
         out_shape=(
-            jax.ShapeDtypeStruct((ROWS, WIDTH), BF16),
-            jax.ShapeDtypeStruct((8, WIDTH), F32),
-            jax.ShapeDtypeStruct((4, WIDTH), F32),
+            pltpu.VMEM((ROWS, WIDTH), BF16),
+            pltpu.VMEM((8, WIDTH), F32),
+            pltpu.VMEM((4, WIDTH), F32),
         ),
         in_specs=[pl.BlockSpec(memory_space=pl.ANY)] * 2 + [vmem] * 2,
         out_specs=(vmem,) * 3,

time: 59.2 us -> 56.8 us (0.959)
  Pallas kernels: 55.5 us -> 54.1 us
  local copies, waits for them, and re-layouts: 2.88 us -> 1.86 us
    pallas_call x1, Pallas kernels: 55.5 us -> 54.1 us  [body(): pl.pallas_call(kernel, out_shape=(pltpu.VMEM((ROWS, WIDTH), BF16), pltpu....]
    unnamed x7 -> x3, local copies, waits for them, and re-layouts: 2.88 us -> 1.86 us
where the time goes in v4:
time: 56.8 us; the launch traced here: 56.6 us
  Pallas kernels  54.1 us (95%)
  local copies, waits for them, and re-layouts  1.86 us (3%)
  between operations  0.64 us (1%)
    pallas_call x1, Pallas kernels, body(): pl.pallas_call(kernel, out_shape=(pltpu.VMEM((ROWS, WIDTH), BF16), pltpu....  54.1 us
    unnamed x3, local copies, waits for them, and re-layouts  1.86 us

profile of v4, /device:TPU:0, one launch (start us, length us, event | category | flops | bytes accessed | tf_op | source)
XLA Modules:
  0.0 56.6 jit_solution(8649809542380213027)
XLA Ops:
  0.6 54.1 %contrastive.1 = (bf16[128,512]{1,0:T(8,128)(2,1)S(1)}, f32[8,512]{1,0:T(8,128)S(1)}, f32[4,512]{1,0:T(4,128)S(1)}) custom-call(bf16[128,1024]{1,0:T(8,128)(2,1)} %feat_hbm.1, bf16[1024,512]{1,0:T(8,128)(2,1)} %wgt_hbm.1, s32[1,128]{1,0:T(1,128)} %bitcast.3, s32[4,128]{1,0:T(4,128)} %bitcast.2), custom_call_target="tpu_custom_call" | custom-call | tf_op jit(solution)/shard_map/contrastive/pallas_call | solution.py:502
  54.7 0.7 %copy.10 = bf16[128,512]{1,0:T(8,128)(2,1)} copy(bf16[128,512]{1,0:T(8,128)(2,1)S(1)} %get-tuple-element.3) | data formatting | bytes 262144
  55.4 0.6 %copy.12 = f32[4,512]{1,0:T(4,128)} copy(f32[4,512]{1,0:T(4,128)S(1)} %get-tuple-element.5) | data formatting | bytes 16384
  56.0 0.6 %copy.11 = f32[8,512]{1,0:T(8,128)} copy(f32[8,512]{1,0:T(8,128)S(1)} %get-tuple-element.4) | data formatting | bytes 32768

commit v5 on v4

--- a/solution.py
+++ b/solution.py
@@ -194,7 +194,7 @@
         copy.wait_send()
     p_ids.update(spread(ucol, my_col, p_dev, (2,)))
     q_ids = {0: spread(ucol, my_col, q_dev, (1, 3))}
-    late_z = [(ulow, spread(ulow, my_row, z_dev))]
+    late_z = [(ulow, spread(ulow, my_row, z_dev, (1, 3)))]
 
     turn = jnp.transpose(feat[...].astype(F32)).reshape(SIDE, SIDE, 2, SIDE, 8, ROWS)
     for z_ in range(SIDE):
@@ -203,7 +203,7 @@
                 for y_ in range(SIDE):
                     feat_t[c_, x_, y_, z_] = turn[z_, x_, c_, y_]
     frow[my_row] = feat_t[...].reshape(FEATURES, ROWS).astype(BF16)
-    late_z.append((frow, spread(frow, my_row, z_dev)))
+    late_z.append((frow, spread(frow, my_row, z_dev, (1, 3))))
 
     for o in RING:
         cp.arrived(lcol.at[col(SIDE - o, 0)], lab_p[o])
@@ -217,11 +217,19 @@
         back = SIDE - o
         cp.arrived(ucol.at[col(back, 0)], p_ids[o])
         q_ids[back] = spread(ucol, col(back, 0), q_dev, (1, 3))
-    q_ids[0].update(spread(ucol, my_col, q_dev, (2,)))
-    for back in (3, 1):
-        q_ids[back].update(spread(ucol, col(back, 0), q_dev, (2,)))
     cp.arrived(ucol.at[col(2, 0)], p_ids[2])
-    q_ids[2] = spread(ucol, col(2, 0), q_dev)
+    q_ids[2] = spread(ucol, col(2, 0), q_dev, (2, 1, 3))
+    low, high = pl.ds(0, ROWS // 2), pl.ds(ROWS // 2, ROWS // 2)
+    far_ids = {}
+
+    def pass_on(o_p):
+        before, after = col(o_p, 3), col(o_p, 1)
+        cp.arrived(ucol.at[before], q_ids[o_p][1])
+        up = cp.send(ucol.at[before, low], ucol.at[before, low], q_dev[1])
+        cp.arrived(ucol.at[after], q_ids[o_p][3])
+        down = cp.send(ucol.at[after, high], ucol.at[after, high], q_dev[3])
+        far_ids[o_p] = (up, down)
+
     for o in RING:
         back = SIDE - o
         cp.arrived(urow.at[row(back)], z_ids[o])
@@ -233,6 +241,8 @@
         line = lcol.at[pl.ds(ring(q, SIDE - o) * SIDE, SIDE)]
         cp.arrived(line, lab_q[o])
     cp.arrived(lrow.at[pl.ds(other * SIDE, SIDE)], lab_s)
+
+    pass_on(0)
 
     lane = lax.broadcasted_iota(jnp.int32, (ROWS, ROWS), 1)
 
@@ -256,6 +266,8 @@
         return carry
 
     lax.fori_loop(0, ROW_BLOCKS, count_block, 0)
+    pass_on(3)
+    pass_on(1)
 
     for o in (0, 3, 1, 2):
         cp.arrived(urow.at[row_sib(o)], sib_ids[o])
@@ -285,9 +297,30 @@
             csum[pl.ds(q_ * SIDE + k, 1), :] = total[:, k * ROWS : (k + 1) * ROWS]
 
     put_sums(q, line_tiles(q, True))
+
+    def ref_halves(ref):
+        n = ref.shape[1] // 2
+        return pl.ds(0, n), pl.ds(n, n)
+
+    late_far = []
+    for (ref, z_sent), (_, s_sent) in zip(late_z, late_s):
+        low_part, high_part = ref_halves(ref)
+        before, after = row(3), row(1)
+        cp.arrived(ref.at[before], z_sent[1])
+        up = cp.send(ref.at[before, low_part], ref.at[before, low_part], z_dev[1])
+        s_sent[3] = cp.send(ref.at[before], ref.at[before], sib)
+        cp.arrived(ref.at[after], z_sent[3])
+        down = cp.send(ref.at[after, high_part], ref.at[after, high_part], z_dev[3])
+        s_sent[1] = cp.send(ref.at[after], ref.at[after], sib)
+        late_far.append((up, down))
+
     for o in RING:
-        for o_p in (0, 3, 1, 2):
-            cp.arrived(ucol.at[col(o_p, SIDE - o)], q_ids[o_p][o])
+        if o == 2:
+            for o_p in (0, 3, 1):
+                far = col(o_p, 2)
+                cp.arrived(ucol.at[far, low], far_ids[o_p][0])
+                cp.arrived(ucol.at[far, high], far_ids[o_p][1])
+        cp.arrived(ucol.at[col(2, SIDE - o)], q_ids[2][o])
         q_ = ring(q, SIDE - o)
         put_sums(q_, line_tiles(q_, False))
 
@@ -333,11 +366,11 @@
     s_part[...] = dot(member, all_keys()).reshape(2, SIDE, 8, WIDTH)
     s_id = cp.send(s_part.at[other], s_recv, sib)
 
-    for (ref, z_sent), (_, s_sent) in zip(late_z, late_s):
-        for o in RING:
-            back = SIDE - o
-            cp.arrived(ref.at[row(back)], z_sent[o])
-            s_sent[back] = cp.send(ref.at[row(back)], ref.at[row(back)], sib)
+    for (ref, s_sent), (up, down) in zip(late_s, late_far):
+        low_part, high_part = ref_halves(ref)
+        cp.arrived(ref.at[row(2), low_part], up)
+        cp.arrived(ref.at[row(2), high_part], down)
+        s_sent[2] = cp.send(ref.at[row(2)], ref.at[row(2)], sib)
     cp.finish()
 
     totals = trow[...]

time: 56.8 us -> 55.9 us (0.984)
  Pallas kernels: 54.1 us -> 53.1 us
    pallas_call x1, Pallas kernels: 54.1 us -> 53.1 us  [body(): pl.pallas_call(kernel, out_shape=(pltpu.VMEM((ROWS, WIDTH), BF16), pltpu....]
where the time goes in v5:
time: 55.9 us; the launch traced here: 55.6 us
  Pallas kernels  53.1 us (95%)
  local copies, waits for them, and re-layouts  1.86 us (3%)
  between operations  0.64 us (1%)
    pallas_call x1, Pallas kernels, body(): pl.pallas_call(kernel, out_shape=(pltpu.VMEM((ROWS, WIDTH), BF16), pltpu....  53.1 us
    unnamed x3, local copies, waits for them, and re-layouts  1.86 us

profile of v5, /device:TPU:0, one launch (start us, length us, event | category | flops | bytes accessed | tf_op | source)
XLA Modules:
  0.0 55.6 jit_solution(13647667224311545297)
XLA Ops:
  0.6 53.1 %contrastive.1 = (bf16[128,512]{1,0:T(8,128)(2,1)S(1)}, f32[8,512]{1,0:T(8,128)S(1)}, f32[4,512]{1,0:T(4,128)S(1)}) custom-call(bf16[128,1024]{1,0:T(8,128)(2,1)} %feat_hbm.1, bf16[1024,512]{1,0:T(8,128)(2,1)} %wgt_hbm.1, s32[1,128]{1,0:T(1,128)} %bitcast.3, s32[4,128]{1,0:T(4,128)} %bitcast.2), custom_call_target="tpu_custom_call" | custom-call | tf_op jit(solution)/shard_map/contrastive/pallas_call | solution.py:535
  53.7 0.7 %copy.10 = bf16[128,512]{1,0:T(8,128)(2,1)} copy(bf16[128,512]{1,0:T(8,128)(2,1)S(1)} %get-tuple-element.3) | data formatting | bytes 262144
  54.4 0.6 %copy.12 = f32[4,512]{1,0:T(4,128)} copy(f32[4,512]{1,0:T(4,128)S(1)} %get-tuple-element.5) | data formatting | bytes 16384
  55.0 0.6 %copy.11 = f32[8,512]{1,0:T(8,128)} copy(f32[8,512]{1,0:T(8,128)S(1)} %get-tuple-element.4) | data formatting | bytes 32768

commit v6 on v5

--- a/solution.py
+++ b/solution.py
@@ -68,13 +68,15 @@
 def kernel(
     feat_hbm,
     wgt_hbm,
-    lab,
-    slots,
+    lab_hbm,
+    slots_hbm,
     pg_out,
     wg_out,
     own_out,
     feat,
     wgt,
+    lab,
+    slots,
     ucol,
     urow,
     ulow,
@@ -151,6 +153,8 @@
     loads = [
         pltpu.make_async_copy(feat_hbm, feat, load_sems.at[0]),
         pltpu.make_async_copy(wgt_hbm, wgt, load_sems.at[1]),
+        pltpu.make_async_copy(lab_hbm, lab, load_sems.at[2]),
+        pltpu.make_async_copy(slots_hbm, slots, load_sems.at[3]),
     ]
     for load in loads:
         load.start()
@@ -218,7 +222,7 @@
         cp.arrived(ucol.at[col(back, 0)], p_ids[o])
         q_ids[back] = spread(ucol, col(back, 0), q_dev, (1, 3))
     cp.arrived(ucol.at[col(2, 0)], p_ids[2])
-    q_ids[2] = spread(ucol, col(2, 0), q_dev, (2, 1, 3))
+    q_ids[2] = spread(ucol, col(2, 0), q_dev, (1, 3))
     low, high = pl.ds(0, ROWS // 2), pl.ds(ROWS // 2, ROWS // 2)
     far_ids = {}
 
@@ -302,6 +306,7 @@
         n = ref.shape[1] // 2
         return pl.ds(0, n), pl.ds(n, n)
 
+    pass_on(2)
     late_far = []
     for (ref, z_sent), (_, s_sent) in zip(late_z, late_s):
         low_part, high_part = ref_halves(ref)
@@ -316,11 +321,10 @@
 
     for o in RING:
         if o == 2:
-            for o_p in (0, 3, 1):
+            for o_p in (0, 3, 1, 2):
                 far = col(o_p, 2)
                 cp.arrived(ucol.at[far, low], far_ids[o_p][0])
                 cp.arrived(ucol.at[far, high], far_ids[o_p][1])
-        cp.arrived(ucol.at[col(2, SIDE - o)], q_ids[2][o])
         q_ = ring(q, SIDE - o)
         put_sums(q_, line_tiles(q_, False))
 
@@ -365,13 +369,6 @@
     member = jnp.where(class_of == lab_lanes, 1.0, 0.0).astype(BF16)
     s_part[...] = dot(member, all_keys()).reshape(2, SIDE, 8, WIDTH)
     s_id = cp.send(s_part.at[other], s_recv, sib)
-
-    for (ref, s_sent), (up, down) in zip(late_s, late_far):
-        low_part, high_part = ref_halves(ref)
-        cp.arrived(ref.at[row(2), low_part], up)
-        cp.arrived(ref.at[row(2), high_part], down)
-        s_sent[2] = cp.send(ref.at[row(2)], ref.at[row(2)], sib)
-    cp.finish()
 
     totals = trow[...]
     for o in t_ids:
@@ -387,6 +384,12 @@
     for o in PLANE:
         cp.arrived(cz.at[o[0] * SIDE + o[1]], c_ids[o])
         col_totals = col_totals + cz[o[0] * SIDE + o[1]]
+    for (ref, s_sent), (up, down) in zip(late_s, late_far):
+        low_part, high_part = ref_halves(ref)
+        cp.arrived(ref.at[row(2), low_part], up)
+        cp.arrived(ref.at[row(2), high_part], down)
+        s_sent[2] = cp.send(ref.at[row(2)], ref.at[row(2)], sib)
+    cp.finish()
     cinv = 1.0 / col_totals
     cinv_lines = [
         jnp.concatenate([cinv[l * SIDE + k : l * SIDE + k + 1, :] for k in range(SIDE)], axis=1)
@@ -410,15 +413,15 @@
         for ref, s_sent in late_s:
             cp.arrived(ref.at[row_sib(o)], s_sent[o])
 
-    for o in range(SIDE):
-        late_wait(o)
-
     for c_, keep in ((other, osib), (c, obuf)):
         rows = pl.ds(pl.multiple_of(c_ * LINE, LINE), LINE)
         part = gradient(rows)
         keep[...] = part
         if keep is osib:
             o_id = cp.send(osib, orecv, sib)
+        if keep is osib:
+            for o in range(SIDE):
+                late_wait(o)
         dpart[rows, :] = project(part, rows, c_ * SIDE, SIDE)
 
     def feats(c_, h):
@@ -493,6 +496,8 @@
     scratch = [
         pltpu.VMEM((ROWS, FEATURES), BF16),
         pltpu.VMEM((FEATURES, WIDTH), BF16),
+        pltpu.VMEM((1, ROWS), jnp.int32),
+        pltpu.VMEM((CLASSES // ROWS, ROWS), jnp.int32),
         pltpu.VMEM((COL_BLOCKS, ROWS, WIDTH), BF16),
         pltpu.VMEM((ROW_BLOCKS, ROWS, WIDTH), BF16),
         pltpu.VMEM((ROW_BLOCKS, ROWS, WIDTH), BF16),
@@ -530,7 +535,7 @@
         pltpu.VMEM((3, 8, WIDTH), F32),
         pltpu.SemaphoreType.DMA((N_COPIES,)),
         pltpu.SemaphoreType.DMA((N_COPIES,)),
-        pltpu.SemaphoreType.DMA((2,)),
+        pltpu.SemaphoreType.DMA((4,)),
     ]
     return pl.pallas_call(
         kernel,
@@ -539,7 +544,7 @@
             pltpu.VMEM((8, WIDTH), F32),
             pltpu.VMEM((4, WIDTH), F32),
         ),
-        in_specs=[pl.BlockSpec(memory_space=pl.ANY)] * 2 + [vmem] * 2,
+        in_specs=[pl.BlockSpec(memory_space=pl.ANY)] * 4,
         out_specs=(vmem,) * 3,
         scratch_shapes=scratch,
         compiler_params=pltpu.CompilerParams(

time: 55.9 us -> 55.2 us (0.987)
  no operation moved by 1% of the time
where the time goes in v6:
time: 55.2 us; the launch traced here: 55.1 us
  Pallas kernels  52.6 us (95%)
  local copies, waits for them, and re-layouts  1.86 us (3%)
  between operations  0.64 us (1%)
    pallas_call x1, Pallas kernels, body(): pl.pallas_call(kernel, out_shape=(pltpu.VMEM((ROWS, WIDTH), BF16), pltpu....  52.6 us
    unnamed x3, local copies, waits for them, and re-layouts  1.86 us

profile of v6, /device:TPU:0, one launch (start us, length us, event | category | flops | bytes accessed | tf_op | source)
XLA Modules:
  0.0 55.1 jit_solution(7924085977417298579)
XLA Ops:
  0.6 52.6 %contrastive.1 = (bf16[128,512]{1,0:T(8,128)(2,1)S(1)}, f32[8,512]{1,0:T(8,128)S(1)}, f32[4,512]{1,0:T(4,128)S(1)}) custom-call(bf16[128,1024]{1,0:T(8,128)(2,1)} %feat_hbm.1, bf16[1024,512]{1,0:T(8,128)(2,1)} %wgt_hbm.1, s32[1,128]{1,0:T(1,128)} %bitcast.3, s32[4,128]{1,0:T(4,128)} %bitcast.2), custom_call_target="tpu_custom_call" | custom-call | tf_op jit(solution)/shard_map/contrastive/pallas_call | solution.py:540
  53.2 0.7 %copy.10 = bf16[128,512]{1,0:T(8,128)(2,1)} copy(bf16[128,512]{1,0:T(8,128)(2,1)S(1)} %get-tuple-element.3) | data formatting | bytes 262144
  53.9 0.6 %copy.12 = f32[4,512]{1,0:T(4,128)} copy(f32[4,512]{1,0:T(4,128)S(1)} %get-tuple-element.5) | data formatting | bytes 16384
  54.5 0.6 %copy.11 = f32[8,512]{1,0:T(8,128)} copy(f32[8,512]{1,0:T(8,128)S(1)} %get-tuple-element.4) | data formatting | bytes 32768
